TPU v7x, 128 devices: a whole 4x4x4 slice. The times are simulated.
128 devices in a mesh: row: 16 (over z_hi, y, core), field: 8 (over z_lo, x).
Axes of the slice: x: 4, y: 4, z: 4 (z_hi: 2, z_lo: 2; z = z_hi * 2 + z_lo), core: 2. Of those that a mesh axis runs over, the one named last changes fastest.
Arguments:
- rhs: bfloat16 [8, 16, 512, 4096], P(None, 'row', None, 'field'), may hold values from -6 to 6
- factor: bfloat16 [8, 16, 512, 1536], P(None, 'row'), may hold values from -0.25 to 0.25
- pivot_map: int32 [1536], replicated, may hold values from 0 to 2, as said below
- pivot_diag: float32 [1536], P('field'), may hold values from -2 to 2, as said below
- pivot_off: float32 [1536], P('field'), may hold values from -4 to 4, as said below
- perm: int32 [3, 512], replicated, may hold values from 0 to 511, each once within a row
Outputs:
- result: float32 [8, 16, 512, 4096], P(None, 'row', None, 'field')
Inputs may be any that keep to these rules, and one draw needn't show every extreme that they name: `pivot_map`: every 1 is followed by a 2 and every 2 follows a 1; no 2x2 block crosses the end of a panel. `pivot_diag`: magnitudes from 1 to 2, either sign. `pivot_off`: magnitudes from 2.5 to 4, either sign.
All inputs are finite; a program needn't handle non-finite values.
Results may differ from a plain program's by a relative error of at most 0.0038.
Values may be sent and summed in bfloat16 or wider, within the bound.
A program may use at most 128 MiB of HBM per device.

v0:
```python
import jax
import jax.numpy as jnp
from jax import lax
from jax.sharding import PartitionSpec as P


def from_root(array, axis, root):
    mine = lax.axis_index(axis) == root
    return lax.psum(jnp.where(mine, array, jnp.zeros_like(array)), axis)


def solve_block(diagonal_block, panel_rows):
    return jax.scipy.linalg.solve_triangular(
        diagonal_block.astype(jnp.float32), panel_rows, lower=True, unit_diagonal=True
    )


def scale_pivots(solved, pivot_codes, diagonal, coupling):
    later_rows = jnp.roll(solved, -1, 0)
    earlier_rows = jnp.roll(solved, 1, 0)
    diagonal_next = jnp.roll(diagonal, -1)
    diagonal_prior = jnp.roll(diagonal, 1)
    coupling_prior = jnp.roll(coupling, 1)
    opens_pair = pivot_codes == 1
    closes_pair = pivot_codes == 2
    self_coef = jnp.where(opens_pair, diagonal_next, jnp.where(closes_pair, diagonal_prior, 1.0))
    next_coef = jnp.where(opens_pair, -coupling, 0.0)
    prior_coef = jnp.where(closes_pair, -coupling_prior, 0.0)
    denominator = jnp.where(
        opens_pair,
        diagonal * diagonal_next - coupling * coupling,
        jnp.where(
            closes_pair, diagonal_prior * diagonal - coupling_prior * coupling_prior, diagonal
        ),
    )
    total_rows = (
        self_coef[:, None] * solved
        + next_coef[:, None] * later_rows
        + prior_coef[:, None] * earlier_rows
    )
    return total_rows / denominator[:, None]


def trailing(factor_cols, solved_low):
    count = factor_cols.shape[0]
    block_size = factor_cols.shape[1]
    depth = factor_cols.shape[2]
    flat = factor_cols.reshape(count * block_size, depth)
    product = jnp.dot(flat, solved_low, preferred_element_type=jnp.float32)
    return product.reshape(count, block_size, solved_low.shape[1])


def local(rhs, factor, pivot_map, pivot_diag, pivot_off, perm):
    row_count = lax.axis_size("row")
    my_row = lax.axis_index("row")
    blocks = rhs.shape[0]
    block_size = rhs.shape[2]
    panels = factor.shape[3] // block_size
    residual_list = [rhs[index, 0].astype(jnp.float32) for index in range(blocks)]
    factor_rows = factor[:, 0]
    diagonal, coupling = (
        lax.all_gather(pivot_diag, "field", axis=0, tiled=True),
        lax.all_gather(pivot_off, "field", axis=0, tiled=True),
    )
    for panel_index in range(panels):
        local_block = panel_index // row_count
        own_rows = residual_list[local_block]
        residual_list[local_block] = jnp.where(
            my_row == panel_index % row_count, own_rows[perm[panel_index]], own_rows
        )
    for panel_index in range(panels):
        owner_row = panel_index % row_count
        local_block = panel_index // row_count
        is_owner = my_row == owner_row
        start = panel_index * block_size
        columns = factor_rows[:, :, start : start + block_size]
        diagonal_block = from_root(columns[local_block], "row", owner_row)
        panel_rows = from_root(residual_list[local_block], "row", owner_row)
        solved = solve_block(diagonal_block, panel_rows)
        solved_low = solved.astype(jnp.bfloat16)
        scaled = scale_pivots(
            solved,
            pivot_map[start : start + block_size],
            diagonal[start : start + block_size],
            coupling[start : start + block_size],
        )
        update = trailing(columns, solved_low)
        for index in range(blocks):
            block_global = index * row_count + my_row
            residual_list[index] = residual_list[index] - jnp.where(
                block_global > panel_index, update[index], 0.0
            )
        residual_list[local_block] = jnp.where(is_owner, scaled, residual_list[local_block])
    return jnp.stack(residual_list, 0)[:, None]


def solution(mesh):
    placed = (
        P(None, "row", None, "field"),
        P(None, "row", None, None),
        P(),
        P("field"),
        P("field"),
        P(),
    )
    return jax.shard_map(
        local, mesh=mesh, in_specs=placed, out_specs=P(None, "row", None, "field"), check_vma=False
    )
```

profile of v0, /device:TPU:116, one launch (start us, length us, event | category | flops | bytes accessed | tf_op | source)
XLA Modules:
  0.0 633.8 jit_solution(10995524944925453019)
XLA Ops:
  6.5 2.6 fusion.71
  11.2 1.6 gather_fusion
  14.0 1.6 gather_fusion.1
  15.9 1.6 gather_fusion.2
  18.9 9.6 %fusion.119 = (bf16[8,512,512]{2,1,0:T(8,128)(2,1)}, bf16[8,512,512]{2,1,0:T(8,128)(2,1)}, bf16[8,512,512]{2,1,0:T(8,128)(2,1)}) fusion(bf16[8,512,1536]{2,1,0:T(8,128)(2,1)} %bitcast.176), kind=kLoop, calls=%fused_computation.233 | loop fusion | bytes 25165824 | tf_op jit(solution)/shard_map/slice | solution.py:76
  30.1 30.0 %all-reduce.2 = (f32[1536]{0:T(1024)S(1)}, f32[1536]{0:T(1024)S(1)}) all-reduce(f32[1536]{0:T(1024)S(1)} %dynamic-update-slice.4, f32[1536]{0:T(1024)S(1)} %dynamic-update-slice.5), channel_id=1, replica_groups=mesh['row'=16,'field'=8] {'field'}, use_global_device_ids=true, to_apply=%add | all-reduce | flops 3072 | bytes 24576
  60.9 3.9 select_select_fusion.5
  64.9 1.9 negate_select_fusion.5
  66.8 2.1 negate_select_fusion.3
  68.8 1.9 negate_select_fusion.1
  70.7 74.4 %all-reduce.15.cloned.1.call-done = (bf16[512,512]{1,0:T(8,128)(2,1)}, bf16[512,512]{1,0:T(8,128)(2,1)}, bf16[512,512]{1,0:T(8,128)(2,1)}) async-done(((bf16[512,512]{1,0:T(8,128)(2,1)}, bf16[512,512]{1,0:T(8,128)(2,1)}, bf16[512,512]{1,0:T(8,128)(2,1)}), (bf16[512,512]{1,0:T(8,128)(2,1)}, bf16[512,512]{1,0:T(8,128)(2,1)}, bf16[512,512]{1,0:T(8,128)(2,1)})) %all-reduce.15.cloned.1.call-update) | async-done | bytes 1572880 | tf_op jit(solution)/shard_map/psum | solution.py:9
  145.1 3.1 convert_add_fusion.2
  148.2 7.5 %while.6 = (s32[]{:T(128)}, f32[512,512]{1,0:T(8,128)S(1)}, s32[4,2]{0,1:T(2,128)S(1)}, f32[4,128,128]{2,1,0:T(8,128)S(1)}, s32[]{:T(128)}) while((s32[]{:T(128)}, f32[512,512]{1,0:T(8,128)S(1)}, s32[4,2]{0,1:T(2,128)S(1)}, f32[4,128,128]{2,1,0:T(8,128)S(1)}, s32[]{:T(128)}) %tuple.107), condition=%wide.while_cond, body=%wide.while_body.sunk | while | flops 2 | bytes 131181 | solution.py:13
  156.5 40.1 %custom-call.5 = f32[4,128,128]{1,2,0:T(8,128)S(1)} custom-call(f32[4,128,128]{2,1,0:T(8,128)} %copy-done.7), custom_call_target="InvertDiagBlocksLowerTriangular" | custom-call | tf_op jit(solution)/shard_map/jit(_solve_triangular)/triangular_solve | solution.py:13
  196.6 93.0 %all-reduce.9.cloned.1.call-done = f32[512,512]{1,0:T(8,128)} async-done(((f32[512,512]{1,0:T(8,128)}), f32[512,512]{1,0:T(8,128)}) %all-reduce.9.cloned.1.call-update) | async-done | bytes 1048592 | tf_op jit(solution)/shard_map/psum | solution.py:9
  289.6 1.5 fusion.88
  294.6 1.6 convolution_subtract_fusion.8
  297.0 2.5 convolution_bitcast_fusion.2
  299.6 2.7 broadcast_select_fusion.1
  303.5 11.1 %while.7 = (s32[]{:T(128)}, f32[512,512]{1,0:T(8,128)}, s32[4,2]{0,1:T(2,128)S(1)}, f32[4,128,128]{2,1,0:T(8,128)S(1)}, s32[]{:T(128)}) while((s32[]{:T(128)}, f32[512,512]{1,0:T(8,128)}, s32[4,2]{0,1:T(2,128)S(1)}, f32[4,128,128]{2,1,0:T(8,128)S(1)}, s32[]{:T(128)}) %tuple.125), condition=%wide.while_cond.clone, body=%wide.while_body.clone.sunk | while | flops 2 | bytes 131181 | solution.py:13
  304.1 2.2 bitcast_dynamic-update-slice_fusion.7
  306.9 2.2 bitcast_dynamic-update-slice_fusion.7
  309.7 2.2 bitcast_dynamic-update-slice_fusion.7
  312.5 2.1 bitcast_dynamic-update-slice_fusion.7
  314.6 39.3 %custom-call.6 = f32[4,128,128]{1,2,0:T(8,128)S(1)} custom-call(f32[4,128,128]{2,1,0:T(8,128)S(1)} %get-tuple-element.27), custom_call_target="InvertDiagBlocksLowerTriangular" | custom-call | tf_op jit(solution)/shard_map/jit(_solve_triangular)/triangular_solve | solution.py:13
  353.9 91.1 %all-reduce.11.cloned.1.call-done = f32[512,512]{1,0:T(8,128)} async-done(((f32[512,512]{1,0:T(8,128)}), f32[512,512]{1,0:T(8,128)}) %all-reduce.11.cloned.1.call-update) | async-done | bytes 1048592 | tf_op jit(solution)/shard_map/psum | solution.py:9
  445.0 1.5 fusion.86
  448.4 1.4 convolution_subtract_fusion.2
  450.2 1.7 convolution_subtract_fusion.7
  452.7 2.3 convolution_bitcast_fusion.1
  455.1 3.2 copy-done.1
  458.3 2.2 broadcast_select_fusion
  460.5 11.8 %while.8 = (s32[]{:T(128)}, f32[512,512]{1,0:T(8,128)}, s32[4,2]{0,1:T(2,128)S(1)}, f32[4,128,128]{2,1,0:T(8,128)S(1)}, s32[]{:T(128)}) while((s32[]{:T(128)}, f32[512,512]{1,0:T(8,128)}, s32[4,2]{0,1:T(2,128)S(1)}, f32[4,128,128]{2,1,0:T(8,128)S(1)}, s32[]{:T(128)}) %tuple.126), condition=%wide.while_cond.clone.1, body=%wide.while_body.clone.1.sunk | while | flops 2 | bytes 131181 | solution.py:13
  461.2 2.3 bitcast_dynamic-update-slice_fusion.8
  464.2 2.3 bitcast_dynamic-update-slice_fusion.8
  467.2 2.3 bitcast_dynamic-update-slice_fusion.8
  470.1 2.2 bitcast_dynamic-update-slice_fusion.8
  472.3 39.6 %custom-call.7 = f32[4,128,128]{1,2,0:T(8,128)S(1)} custom-call(f32[4,128,128]{2,1,0:T(8,128)S(1)} %get-tuple-element.28), custom_call_target="InvertDiagBlocksLowerTriangular" | custom-call | tf_op jit(solution)/shard_map/jit(_solve_triangular)/triangular_solve | solution.py:13
  511.9 90.5 %all-reduce.13.cloned.1.call-done = f32[512,512]{1,0:T(8,128)} async-done(((f32[512,512]{1,0:T(8,128)}), f32[512,512]{1,0:T(8,128)}) %all-reduce.13.cloned.1.call-update) | async-done | bytes 1048592 | tf_op jit(solution)/shard_map/psum | solution.py:9
  602.5 1.5 fusion.84
  605.8 1.4 convolution_subtract_fusion
  607.7 1.7 convolution_subtract_fusion.6
  610.2 2.3 convolution_bitcast_fusion
  612.5 1.4 fusion.38
  619.0 1.4 fusion.27
  620.4 1.4 fusion.22
  621.8 1.4 fusion.17
  623.1 1.4 fusion.12
  (117 shorter events, 39.0 us)
Async XLA Ops:
  6.5 138.6 %all-reduce.15.cloned.1.call-start = ((), (), s32[]{:S(2)}) async-start(), calls=%async_computation.3 | async-start | bytes 3145728 | tf_op jit(solution)/shard_map/psum | solution.py:9
  9.1 280.4 %all-reduce.9.cloned.1.call-start = ((), (), s32[]{:S(2)}) async-start(), calls=%async_computation | async-start | bytes 2097152 | tf_op jit(solution)/shard_map/psum | solution.py:9
  18.8 426.3 %all-reduce.11.cloned.1.call-start = ((), (), s32[]{:S(2)}) async-start(), calls=%async_computation.1 | async-start | bytes 2097152 | tf_op jit(solution)/shard_map/psum | solution.py:9
  18.8 9.6 %copy-start.11 = (u32[128]{0:T(128)S(1)}, u32[128]{0:T(128)}, u32[]{:S(2)}) copy-start(u32[128]{0:T(128)} %constant.73) | copy-start | bytes 1540
  18.8 10.8 %copy-start.9 = (f32[192]{0:T(256)S(1)}, f32[192]{0:T(256)}, u32[]{:S(2)}) copy-start(f32[192]{0:T(256)} %param.11) | copy-start | bytes 2308
  18.9 11.1 %copy-start.10 = (f32[192]{0:T(256)S(1)}, f32[192]{0:T(256)}, u32[]{:S(2)}) copy-start(f32[192]{0:T(256)} %param.12) | copy-start | bytes 2308
  18.9 42.1 %copy-start.8 = (s32[1536]{0:T(1024)S(1)}, s32[1536]{0:T(1024)}, u32[]{:S(2)}) copy-start(s32[1536]{0:T(1024)} %param.10) | copy-start | bytes 18436
  155.8 0.7 copy-start.7
  289.6 7.4 %copy-start.4 = (bf16[8,512,512]{2,1,0:T(8,128)(2,1)S(1)}, bf16[8,512,512]{2,1,0:T(8,128)(2,1)}, u32[]{:S(2)}) copy-start(bf16[8,512,512]{2,1,0:T(8,128)(2,1)} %get-tuple-element.79) | copy-start | bytes 12582916
  299.6 3.6 copy-start
  303.2 299.2 %all-reduce.13.cloned.1.call-start = ((), (), s32[]{:S(2)}) async-start(), calls=%async_computation.2 | async-start | bytes 2097152 | tf_op jit(solution)/shard_map/psum | solution.py:9
  445.0 7.7 %copy-start.3 = (bf16[8,512,512]{2,1,0:T(8,128)(2,1)S(1)}, bf16[8,512,512]{2,1,0:T(8,128)(2,1)}, u32[]{:S(2)}) copy-start(bf16[8,512,512]{2,1,0:T(8,128)(2,1)} %get-tuple-element.78) | copy-start | bytes 12582916
  455.0 3.2 copy-start.1
  602.5 7.7 %copy-start.2 = (bf16[8,512,512]{2,1,0:T(8,128)(2,1)S(1)}, bf16[8,512,512]{2,1,0:T(8,128)(2,1)}, u32[]{:S(2)}) copy-start(bf16[8,512,512]{2,1,0:T(8,128)(2,1)} %get-tuple-element.77) | copy-start | bytes 12582916
  609.9 4.1 slice-start
  609.9 4.1 slice-start.2
  610.1 2.4 copy-start.6
  610.2 5.1 slice-start.1
  610.2 6.3 slice-start.3
  610.2 7.4 %copy-start.5 = (bf16[8,1,512,512]{3,2,1,0:T(8,128)(2,1)S(1)}, bf16[8,1,512,512]{3,2,1,0:T(8,128)(2,1)}, u32[]{:S(2)}) copy-start(bf16[8,1,512,512]{3,2,1,0:T(8,128)(2,1)} %param.8) | copy-start | bytes 12582916
Sparse Core Ops, SparseCore 0:
  10.1 134.9 all-reduce.14
  147.7 141.7 all-reduce.8
  303.3 141.6 all-reduce.10
  460.6 141.7 all-reduce.12
where the time goes:
time: 646 us; the launch traced here: 634 us
  waiting for transfers between devices  349 us (54%)
  other arithmetic  155 us (24%)
  local copies, waits for them, and re-layouts  55.7 us (9%)
  blocking collectives  30 us (5%)
  matrix products  28.8 us (4%)
  between operations  14.3 us (2%)
    psum x4, waiting for transfers between devices, from_root(): return lax.psum(jnp.where(mine, array, jnp.zeros_like(array)), axis)  349 us
    another operation x9, other arithmetic, solve_block(): jax.scipy.linalg.solve_triangular(diagonal_block.astype(jnp.float32), pan...  122 us
    another operation x40, local copies, waits for them, and re-layouts, solve_block(): jax.scipy.linalg.solve_triangular(diagonal_block.astype(jnp.float32), pan...  30.2 us
    unnamed x1, blocking collectives  30 us
    another operation x21, matrix products, solve_block(): jax.scipy.linalg.solve_triangular(diagonal_block.astype(jnp.float32), pan...  21.6 us
  transfers between devices with their start and end apart: 4, of which 4 were waited for; matrix products, arithmetic and copies ran while one was open for 29% of the time, Pallas kernels for 0%

commit v1 on v0

v1 whole, which is shorter than its diff:
```python
import jax
import jax.numpy as jnp
from jax import lax
from jax.experimental import pallas as pl
from jax.experimental.pallas import tpu as pltpu
from jax.sharding import PartitionSpec as P

MESH = pl.DeviceIdType.MESH
F32, BF16 = jnp.float32, jnp.bfloat16
NB, PANELS, BLOCKS = 512, 3, 8
HALF = 256
CHUNK = 128
CHUNKS = 4
FIELDS, ROWS = 8, 16
DPART = 192


def dot(a, b):
    return jnp.dot(a, b, preferred_element_type=F32)


def split(a):
    high = a.astype(BF16)
    return high, (a - high.astype(F32)).astype(BF16)


def dot2(a, b):
    return dot(a[0], b) + dot(a[1], b)


def dot2r(a, b):
    return dot(a, b[0]) + dot(a, b[1])


def dot3(a, b):
    return dot(a[0], b[0]) + (dot(a[0], b[1]) + dot(a[1], b[0]))


def invert_tiles(tiles):
    rows = lax.broadcasted_iota(jnp.int32, (256, 256), 0)
    cols = lax.broadcasted_iota(jnp.int32, (256, 256), 1)
    eye = jnp.where(rows == cols, 1.0, 0.0)
    base = (rows > cols) & (rows // 16 == cols // 16)
    n1 = [jnp.where(base, t, 0.0) for t in tiles]
    n1b = [n.astype(BF16) for n in n1]
    n2 = [dot(n, n) for n in n1b]
    n2s = [split(n) for n in n2]
    n4 = [dot3(s, s) for s in n2s]
    x = [eye - a + b - dot2r(ab, bs) for a, b, ab, bs in zip(n1, n2, n1b, n2s)]
    n4s = [split(n) for n in n4]
    n8s = [split(dot3(s, s)) for s in n4s]
    x = [a + dot3(split(a), s) for a, s in zip(x, n4s)]
    x = [a + dot3(split(a), s) for a, s in zip(x, n8s)]
    size = 16
    while size < 256:
        off = (rows // (2 * size) == cols // (2 * size)) & (rows // size > cols // size)
        es = [jnp.where(off, t, 0.0).astype(BF16) for t in tiles]
        xs = [split(a) for a in x]
        ys = [split(dot2r(e, s)) for e, s in zip(es, xs)]
        x = [a - dot3(s, y) for a, s, y in zip(x, xs, ys)]
        size *= 2
    return x


def kernel(rhs, factor, pmap, pdiag, poff, perm, out, fac, b, w, xh, xl, c, m0h, m0l, m1h, m1l,
           coef, dsend, dall, load_sem, send_sem, recv_sem, core_sem, dsend_sem, drecv_sem):
    r = lax.axis_index("row")
    f = lax.axis_index("field")
    solver = r < PANELS
    mate = r + 1 - 2 * lax.rem(r, 2)

    barrier = pltpu.get_barrier_semaphore()
    for k in range(1, ROWS):
        pl.semaphore_signal(barrier, inc=1, device_id=(lax.rem(r + k, ROWS), f), device_id_type=MESH)

    @pl.when(solver)
    def _():
        for k in range(1, FIELDS):
            pl.semaphore_signal(barrier, inc=1, device_id=(r, lax.rem(f + k, FIELDS)), device_id_type=MESH)

    loads = []
    for l in range(BLOCKS):
        loads.append(pltpu.make_async_copy(factor.at[l, 0], fac.at[l], load_sem.at[0, l]))
        loads.append(pltpu.make_async_copy(rhs.at[l, 0], b.at[l], load_sem.at[1, l]))
        loads[-2].start()
        loads[-1].start()

    def wslot(p, j):
        return w.at[p, j // 2, :, pl.ds((j % 2) * CHUNK, CHUNK)]

    def send(p, j, k, dst):
        return pltpu.make_async_remote_copy(
            wslot(p, j), wslot(p, j), send_sem.at[p, j, k], recv_sem.at[p, j],
            device_id=(dst, f), device_id_type=MESH)

    def to_mate(p, j):
        return pltpu.make_async_remote_copy(
            wslot(p, j), wslot(p, j), core_sem.at[p, j], recv_sem.at[p, j],
            device_id=(mate, f), device_id_type=MESH)

    ICI = [
        [(0, (2, 6, 8)), (2, (4,)), (8, (10, 14)), (10, (12,))],
        [(1, (2, 6, 8)), (2, (4,)), (8, (10, 14)), (10, (12,))],
        [(2, (10, 0, 6, 4)), (10, (14, 8, 12))],
    ]

    def core_sender(p):
        even = lax.rem(r, 2) == 0
        if p == 1:
            return (r == 1) | (even & (r > 0))
        return even

    def forward(p, j):
        for src, dsts in ICI[p]:
            @pl.when(r == src)
            def _():
                for k, dst in enumerate(dsts):
                    send(p, j, k, dst).start()

        @pl.when(core_sender(p))
        def _():
            to_mate(p, j).start()

    def arrive(p, j):
        @pl.when(r != p)
        def _():
            to_mate(p, j).wait_recv()

    loads[0].wait()
    loads[1].wait()

    @pl.when(solver)
    def _():
        own = pl.multiple_of(r * NB, NB)
        tiles = [fac[0, t * 256:(t + 1) * 256, pl.ds(own + t * 256, 256)].astype(F32) for t in range(2)]
        x11, x22 = invert_tiles(tiles)
        l21 = fac[0, 256:512, pl.ds(own, 256)]
        x11s, x22s = split(x11), split(x22)
        x21s = split(-dot3(x22s, split(dot2r(l21, x11s))))
        zero = jnp.zeros((256, 256), BF16)
        for ref, k in ((xh, 0), (xl, 1)):
            ref[0:256, 0:256] = x11s[k]
            ref[0:256, 256:512] = zero
            ref[256:512, 0:256] = x21s[k]
            ref[256:512, 256:512] = x22s[k]

        def apply_x(right):
            top = dot(xh[0:256, 0:256], right[0:256]) + dot(xl[0:256, 0:256], right[0:256])
            low = dot(xh[256:512, :], right) + dot(xl[256:512, :], right)
            return top, low

        dsend[...] = jnp.zeros_like(dsend)
        dsend[0:1, 0:DPART] = pdiag[...].reshape(1, DPART)
        dsend[1:2, 0:DPART] = poff[...].reshape(1, DPART)

        which = lax.broadcasted_iota(jnp.int32, (128, NB), 0)
        prow = jnp.where(r == 0, perm[0:1, :], jnp.where(r == 1, perm[1:2, :], perm[2:3, :]))
        pcol = jnp.where(which == 0, prow.astype(F32), 0.0).T[:, 0:1].astype(jnp.int32)
        onehot = jnp.where(lax.broadcasted_iota(jnp.int32, (NB, NB), 1) == pcol, 1.0, 0.0).astype(BF16)
        pb = dot(onehot, b[0]).astype(BF16)
        top, low = apply_x(pb)
        c[0:256, :] = top
        c[256:512, :] = low

        @pl.when(r >= 1)
        def _():
            for k, part in enumerate(apply_x(fac[0, :, 0:NB])):
                m0h[k * 256:(k + 1) * 256, :], m0l[k * 256:(k + 1) * 256, :] = split(part)

        @pl.when(r >= 2)
        def _():
            for k, part in enumerate(apply_x(fac[0, :, NB:2 * NB])):
                m1h[k * 256:(k + 1) * 256, :], m1l[k * 256:(k + 1) * 256, :] = split(part)

    @pl.when(solver)
    def _():
        pl.semaphore_wait(barrier, ROWS - 1 + FIELDS - 1)

    @pl.when(jnp.logical_not(solver))
    def _():
        pl.semaphore_wait(barrier, ROWS - 1)

    def cols(j):
        return slice(j * CHUNK, (j + 1) * CHUNK)

    def wcols(p, j):
        return w[p, j // 2, :, (j % 2) * CHUNK:(j % 2 + 1) * CHUNK]

    def emit(p, j, z):
        out[0, 0, :, cols(j)] = z
        w[p, j // 2, :, (j % 2) * CHUNK:(j % 2 + 1) * CHUNK] = z.astype(BF16)

    def trailing01(h):
        first = jnp.where(solver, 1, 0)
        sl = slice(h * HALF, (h + 1) * HALF)

        def step(l, carry):
            out[l, 0, :, sl] = b[l, :, sl].astype(F32) - (
                dot(fac[l, :, 0:NB], w[0, h]) + dot(fac[l, :, NB:2 * NB], w[1, h]))
            return carry
        lax.fori_loop(first, BLOCKS, step, 0)

    def trailing2(h):
        first = jnp.where(solver, 1, 0)
        sl = slice(h * HALF, (h + 1) * HALF)

        def step(l, carry):
            out[l, 0, :, sl] = out[l, 0, :, sl] - dot(fac[l, :, 2 * NB:3 * NB], w[2, h])
            return carry
        lax.fori_loop(first, BLOCKS, step, 0)

    def rest_loaded():
        for copy in loads[2:]:
            copy.wait()

    for j in range(CHUNKS):
        @pl.when(r == 0)
        def _():
            emit(0, j, c[:, cols(j)])
        arrive(0, j)
        forward(0, j)

        @pl.when(r == 1)
        def _():
            wj = wcols(0, j)
            emit(1, j, c[:, cols(j)] - (dot(m0h[...], wj) + dot(m0l[...], wj)))

        @pl.when(r != 0)
        def _():
            arrive(1, j)
            forward(1, j)

        @pl.when(r == 2)
        def _():
            w0, w1 = wcols(0, j), wcols(1, j)
            emit(2, j, c[:, cols(j)] - ((dot(m0h[...], w0) + dot(m0l[...], w0))
                                       + (dot(m1h[...], w1) + dot(m1l[...], w1))))
            forward(2, j)

    @pl.when(r == 0)
    def _():
        for j in range(CHUNKS):
            arrive(1, j)

    def dcopy(k):
        return pltpu.make_async_remote_copy(
            dsend, dall.at[f], dsend_sem.at[k], drecv_sem.at[f],
            device_id=(r, lax.rem(f + k, FIELDS)), device_id_type=MESH)

    def darrival(k):
        src = lax.rem(f + k, FIELDS)
        return pltpu.make_async_remote_copy(
            dsend, dall.at[src], dsend_sem.at[k], drecv_sem.at[src],
            device_id=(r, src), device_id_type=MESH)

    @pl.when(solver)
    def _():
        for k in range(1, FIELDS):
            dcopy(k).start()

    rest_loaded()
    trailing01(0)
    trailing01(1)

    for j in range(CHUNKS):
        @pl.when(r != 2)
        def _():
            arrive(2, j)
            forward(2, j)
        if j == 1:
            trailing2(0)

    trailing2(1)

    @pl.when(solver)
    def _():
        for k in range(1, FIELDS):
            darrival(k).wait_recv()
        for k in range(1, FIELDS):
            dcopy(k).wait_send()
        wide = jnp.zeros((8, PANELS * NB), F32)
        pad = jnp.zeros((8, PANELS * NB - 256), F32)
        for k in range(FIELDS):
            part = jnp.where(f == k, dsend[...], dall[k])
            row = jnp.concatenate([part, pad], axis=1)
            wide = wide + (pltpu.roll(row, k * DPART, 1) if k else row)

        def mine(a):
            return jnp.where(r == 0, a[:, 0:NB], jnp.where(r == 1, a[:, NB:2 * NB], a[:, 2 * NB:3 * NB]))
        both = mine(wide)
        diag, off = both[0:1], both[1:2]
        code = mine(pmap[...].reshape(1, PANELS * NB))
        diag8 = jnp.broadcast_to(diag, (8, NB))
        off8 = jnp.broadcast_to(off, (8, NB))
        code8 = jnp.broadcast_to(code, (8, NB))
        after, before = pltpu.roll(diag8, NB - 1, 1), pltpu.roll(diag8, 1, 1)
        off_before = pltpu.roll(off8, 1, 1)
        opens, closes = code8 == 1, code8 == 2
        den = jnp.where(opens, diag8 * after - off8 * off8,
                        jnp.where(closes, before * diag8 - off_before * off_before, diag8))
        own_c = jnp.where(opens, after, jnp.where(closes, before, 1.0)) / den
        next_c = jnp.where(opens, -off8, 0.0) / den
        prior_c = jnp.where(closes, -off_before, 0.0) / den
        which = lax.broadcasted_iota(jnp.int32, (128, NB), 0)
        stack = jnp.where(which == 0, own_c[0:1], jnp.where(which == 1, next_c[0:1],
                          jnp.where(which == 2, prior_c[0:1], 0.0)))
        coef[...] = stack.T
        own_k, next_k, prior_k = coef[:, 0:1], coef[:, 1:2], coef[:, 2:3]
        for j in range(CHUNKS):
            z = out[0, 0, :, cols(j)]
            out[0, 0, :, cols(j)] = (own_k * z + next_k * pltpu.roll(z, NB - 1, 0)
                                     + prior_k * pltpu.roll(z, 1, 0))

    for p in range(PANELS):
        for j in range(CHUNKS):
            for src, dsts in ICI[p]:
                @pl.when(r == src)
                def _():
                    for k, dst in enumerate(dsts):
                        send(p, j, k, dst).wait_send()

            @pl.when(core_sender(p))
            def _():
                to_mate(p, j).wait_send()


def local(rhs, factor, pivot_map, pivot_diag, pivot_off, perm):
    vmem = pl.BlockSpec(memory_space=pltpu.VMEM)
    hbm = pl.BlockSpec(memory_space=pltpu.HBM)
    return pl.pallas_call(
        kernel,
        out_shape=jax.ShapeDtypeStruct((BLOCKS, 1, NB, NB), F32),
        in_specs=[hbm, hbm, vmem, vmem, vmem, vmem],
        out_specs=vmem,
        scratch_shapes=[
            pltpu.VMEM((BLOCKS, NB, PANELS * NB), BF16),
            pltpu.VMEM((BLOCKS, NB, NB), BF16),
            pltpu.VMEM((PANELS, 2, NB, HALF), BF16),
            pltpu.VMEM((NB, NB), BF16), pltpu.VMEM((NB, NB), BF16),
            pltpu.VMEM((NB, NB), F32),
            pltpu.VMEM((NB, NB), BF16), pltpu.VMEM((NB, NB), BF16),
            pltpu.VMEM((NB, NB), BF16), pltpu.VMEM((NB, NB), BF16),
            pltpu.VMEM((NB, 128), F32),
            pltpu.VMEM((8, 256), F32), pltpu.VMEM((FIELDS, 8, 256), F32),
            pltpu.SemaphoreType.DMA((2, BLOCKS)),
            pltpu.SemaphoreType.DMA((PANELS, CHUNKS, 4)),
            pltpu.SemaphoreType.DMA((PANELS, CHUNKS)),
            pltpu.SemaphoreType.DMA((PANELS, CHUNKS)),
            pltpu.SemaphoreType.DMA((FIELDS,)), pltpu.SemaphoreType.DMA((FIELDS,)),
        ],
        compiler_params=pltpu.CompilerParams(
            collective_id=0, has_side_effects=True, vmem_limit_bytes=38 << 20),
        cost_estimate=pl.CostEstimate(flops=2 * 4096 * 1536 * 512, bytes_accessed=24 << 20, transcendentals=0),
    )(rhs, factor, pivot_map, pivot_diag, pivot_off, perm)


def solution(mesh):
    placed = (
        P(None, "row", None, "field"),
        P(None, "row", None, None),
        P(),
        P("field"),
        P("field"),
        P(),
    )
    return jax.shard_map(
        local, mesh=mesh, in_specs=placed, out_specs=P(None, "row", None, "field"), check_vma=False
    )
```

time: 646 us -> 60 us (0.09)
  the two profiles are of different devices: /device:TPU:116 before, /device:TPU:103 now
where the time goes in v1:
time: 60 us; the launch traced here: 59.7 us
  Pallas kernels  51.4 us (86%)
  local copies, waits for them, and re-layouts  8.34 us (14%)
    pallas_call x1, Pallas kernels, local(): pl.pallas_call(kernel, out_shape=jax.ShapeDtypeStruct((BLOCKS, 1, NB, NB)...  51.4 us
    unnamed x11, local copies, waits for them, and re-layouts  8.34 us

profile of v1, /device:TPU:103, one launch (start us, length us, event | category | flops | bytes accessed | tf_op | source)
XLA Modules:
  0.0 59.7 jit_solution(14520239341443542705)
XLA Ops:
  0.0 0.0 copy-start
  0.0 2.2 %copy-done = bf16[8,1,512,512]{3,2,1,0:T(8,128)(2,1)S(1)} copy-done((bf16[8,1,512,512]{3,2,1,0:T(8,128)(2,1)S(1)}, bf16[8,1,512,512]{3,2,1,0:T(8,128)(2,1)}, u32[]{:S(2)}) %copy-start) | copy-done | bytes 4194328
  2.2 0.0 copy-start.1
  2.2 0.7 %copy-done.1 = s32[1536]{0:T(1024)S(1)} copy-done((s32[1536]{0:T(1024)S(1)}, s32[1536]{0:T(1024)}, u32[]{:S(2)}) %copy-start.1) | copy-done | bytes 6168
  2.9 0.0 copy-start.2
  2.9 0.7 %copy-done.2 = s32[3,512]{1,0:T(4,128)S(1)} copy-done((s32[3,512]{1,0:T(4,128)S(1)}, s32[3,512]{1,0:T(4,128)}, u32[]{:S(2)}) %copy-start.2) | copy-done | bytes 6168
  3.6 0.0 copy-start.3
  3.6 0.7 %copy-done.3 = f32[192]{0:T(256)S(1)} copy-done((f32[192]{0:T(256)S(1)}, f32[192]{0:T(256)}, u32[]{:S(2)}) %copy-start.3) | copy-done | bytes 792
  4.3 0.0 copy-start.4
  4.3 0.7 %copy-done.4 = f32[192]{0:T(256)S(1)} copy-done((f32[192]{0:T(256)S(1)}, f32[192]{0:T(256)}, u32[]{:S(2)}) %copy-start.4) | copy-done | bytes 792
  4.9 51.4 %shard_map.64 = f32[8,1,512,512]{3,2,1,0:T(8,128)S(1)} custom-call(bf16[8,1,512,512]{3,2,1,0:T(8,128)(2,1)S(1)} %copy-done, bf16[8,1,512,1536]{3,2,1,0:T(8,128)(2,1)} %factor.1, s32[1536]{0:T(1024)S(1)} %copy-done.1, f32[192]{0:T(256)S(1)} %copy-done.3, f32[192]{0:T(256)S(1)} %copy-done.4, s32[3,512]{1,0:T(4,128)S(1)} %copy-done.2), custom_call_target="tpu_custom_call" | custom-call | flops 6442450944 | bytes 25165824 | tf_op jit(solution)/shard_map/pallas_call | solution.py:330
  56.3 3.4 %copy.8 = f32[8,1,512,512]{3,2,1,0:T(8,128)} copy(f32[8,1,512,512]{3,2,1,0:T(8,128)S(1)} %shard_map.64) | data formatting | bytes 16777216
Async XLA Ops:
  0.0 2.2 %copy-start = (bf16[8,1,512,512]{3,2,1,0:T(8,128)(2,1)S(1)}, bf16[8,1,512,512]{3,2,1,0:T(8,128)(2,1)}, u32[]{:S(2)}) copy-start(bf16[8,1,512,512]{3,2,1,0:T(8,128)(2,1)} %rhs.1) | copy-start | bytes 12582916
  2.2 0.7 %copy-start.1 = (s32[1536]{0:T(1024)S(1)}, s32[1536]{0:T(1024)}, u32[]{:S(2)}) copy-start(s32[1536]{0:T(1024)} %pmap.1) | copy-start | bytes 18436
  2.9 0.7 %copy-start.2 = (s32[3,512]{1,0:T(4,128)S(1)}, s32[3,512]{1,0:T(4,128)}, u32[]{:S(2)}) copy-start(s32[3,512]{1,0:T(4,128)} %perm.1) | copy-start | bytes 18436
  3.6 0.7 %copy-start.3 = (f32[192]{0:T(256)S(1)}, f32[192]{0:T(256)}, u32[]{:S(2)}) copy-start(f32[192]{0:T(256)} %pdiag.1) | copy-start | bytes 2308
  4.3 0.7 %copy-start.4 = (f32[192]{0:T(256)S(1)}, f32[192]{0:T(256)}, u32[]{:S(2)}) copy-start(f32[192]{0:T(256)} %poff.1) | copy-start | bytes 2308

commit v2 on v1

--- a/solution.py
+++ b/solution.py
@@ -62,28 +62,35 @@
     return x
 
 
-def kernel(rhs, factor, pmap, pdiag, poff, perm, out, fac, b, w, xh, xl, c, m0h, m0l, m1h, m1l,
-           coef, dsend, dall, load_sem, send_sem, recv_sem, core_sem, dsend_sem, drecv_sem):
+def kernel(rhs, factor, pmap_hbm, pdiag_hbm, poff_hbm, perm_hbm, out, fac, b, w, xh, xl, c,
+           m0h, m0l, m1h, m1l, coef, dsend, dall, pmap, pdiag, poff, perm,
+           load_sem, small_sem, send_sem, recv_sem, core_sem, dsend_sem, drecv_sem):
     r = lax.axis_index("row")
     f = lax.axis_index("field")
+    even = lax.rem(r, 2) == 0
+    odd = jnp.logical_not(even)
     solver = r < PANELS
     mate = r + 1 - 2 * lax.rem(r, 2)
-
-    barrier = pltpu.get_barrier_semaphore()
-    for k in range(1, ROWS):
-        pl.semaphore_signal(barrier, inc=1, device_id=(lax.rem(r + k, ROWS), f), device_id_type=MESH)
-
-    @pl.when(solver)
-    def _():
-        for k in range(1, FIELDS):
-            pl.semaphore_signal(barrier, inc=1, device_id=(r, lax.rem(f + k, FIELDS)), device_id_type=MESH)
 
     loads = []
     for l in range(BLOCKS):
         loads.append(pltpu.make_async_copy(factor.at[l, 0], fac.at[l], load_sem.at[0, l]))
         loads.append(pltpu.make_async_copy(rhs.at[l, 0], b.at[l], load_sem.at[1, l]))
-        loads[-2].start()
-        loads[-1].start()
+    small = [pltpu.make_async_copy(src, dst, small_sem.at[k]) for k, (src, dst) in enumerate(
+        ((perm_hbm, perm), (pmap_hbm, pmap), (pdiag_hbm, pdiag), (poff_hbm, poff)))]
+    loads[0].start()
+    for copy in small:
+        copy.start()
+    loads[1].start()
+
+    barrier = pltpu.get_barrier_semaphore()
+    for k in range(1, ROWS):
+        pl.semaphore_signal(barrier, inc=1, device_id=(lax.rem(r + k, ROWS), f), device_id_type=MESH)
+
+    @pl.when(solver)
+    def _():
+        for k in range(1, FIELDS):
+            pl.semaphore_signal(barrier, inc=1, device_id=(r, lax.rem(f + k, FIELDS)), device_id_type=MESH)
 
     def wslot(p, j):
         return w.at[p, j // 2, :, pl.ds((j % 2) * CHUNK, CHUNK)]
@@ -98,39 +105,41 @@
             wslot(p, j), wslot(p, j), core_sem.at[p, j], recv_sem.at[p, j],
             device_id=(mate, f), device_id_type=MESH)
 
-    ICI = [
-        [(0, (2, 6, 8)), (2, (4,)), (8, (10, 14)), (10, (12,))],
-        [(1, (2, 6, 8)), (2, (4,)), (8, (10, 14)), (10, (12,))],
-        [(2, (10, 0, 6, 4)), (10, (14, 8, 12))],
-    ]
+    EARLY = ((6, (4, 14)), (4, (12,)), (8, (10,)))
+    ICI = [((0, (2, 6, 8)),) + EARLY, ((1, (2, 6, 8)),) + EARLY,
+           ((2, (11, 1, 5)), (1, (7, 9)), (11, (15, 13)))]
 
     def core_sender(p):
-        even = lax.rem(r, 2) == 0
+        if p == 0:
+            return even
         if p == 1:
             return (r == 1) | (even & (r > 0))
-        return even
-
-    def forward(p, j):
+        return (r == 2) | (odd & (r != 3))
+
+    def forward(p, j, *rows):
         for src, dsts in ICI[p]:
-            @pl.when(r == src)
-            def _():
-                for k, dst in enumerate(dsts):
-                    send(p, j, k, dst).start()
-
-        @pl.when(core_sender(p))
-        def _():
-            to_mate(p, j).start()
+            if src in rows:
+                @pl.when(r == src)
+                def _():
+                    for k, dst in enumerate(dsts):
+                        send(p, j, k, dst).start()
 
     def arrive(p, j):
-        @pl.when(r != p)
-        def _():
-            to_mate(p, j).wait_recv()
-
-    loads[0].wait()
-    loads[1].wait()
+        to_mate(p, j).wait_recv()
+
+    for copy in small + loads[:2]:
+        copy.wait()
+    for copy in loads[2:]:
+        copy.start()
 
     @pl.when(solver)
     def _():
+        which = lax.broadcasted_iota(jnp.int32, (128, NB), 0)
+        prow = jnp.where(r == 0, perm[0:1, :], jnp.where(r == 1, perm[1:2, :], perm[2:3, :]))
+        pcol = jnp.where(which == 0, prow.astype(F32), 0.0).T[:, 0:1].astype(jnp.int32)
+        onehot = jnp.where(lax.broadcasted_iota(jnp.int32, (NB, NB), 1) == pcol, 1.0, 0.0).astype(BF16)
+        pb = dot(onehot, b[0]).astype(BF16)
+
         own = pl.multiple_of(r * NB, NB)
         tiles = [fac[0, t * 256:(t + 1) * 256, pl.ds(own + t * 256, 256)].astype(F32) for t in range(2)]
         x11, x22 = invert_tiles(tiles)
@@ -149,15 +158,6 @@
             low = dot(xh[256:512, :], right) + dot(xl[256:512, :], right)
             return top, low
 
-        dsend[...] = jnp.zeros_like(dsend)
-        dsend[0:1, 0:DPART] = pdiag[...].reshape(1, DPART)
-        dsend[1:2, 0:DPART] = poff[...].reshape(1, DPART)
-
-        which = lax.broadcasted_iota(jnp.int32, (128, NB), 0)
-        prow = jnp.where(r == 0, perm[0:1, :], jnp.where(r == 1, perm[1:2, :], perm[2:3, :]))
-        pcol = jnp.where(which == 0, prow.astype(F32), 0.0).T[:, 0:1].astype(jnp.int32)
-        onehot = jnp.where(lax.broadcasted_iota(jnp.int32, (NB, NB), 1) == pcol, 1.0, 0.0).astype(BF16)
-        pb = dot(onehot, b[0]).astype(BF16)
         top, low = apply_x(pb)
         c[0:256, :] = top
         c[256:512, :] = low
@@ -172,8 +172,6 @@
             for k, part in enumerate(apply_x(fac[0, :, NB:2 * NB])):
                 m1h[k * 256:(k + 1) * 256, :], m1l[k * 256:(k + 1) * 256, :] = split(part)
 
-    @pl.when(solver)
-    def _():
         pl.semaphore_wait(barrier, ROWS - 1 + FIELDS - 1)
 
     @pl.when(jnp.logical_not(solver))
@@ -190,57 +188,90 @@
         out[0, 0, :, cols(j)] = z
         w[p, j // 2, :, (j % 2) * CHUNK:(j % 2 + 1) * CHUNK] = z.astype(BF16)
 
+    def on_blocks(step):
+        pl.when(jnp.logical_not(solver))(lambda: step(0))
+        for l in range(1, BLOCKS):
+            step(l)
+
     def trailing01(h):
-        first = jnp.where(solver, 1, 0)
         sl = slice(h * HALF, (h + 1) * HALF)
 
-        def step(l, carry):
+        def step(l):
             out[l, 0, :, sl] = b[l, :, sl].astype(F32) - (
                 dot(fac[l, :, 0:NB], w[0, h]) + dot(fac[l, :, NB:2 * NB], w[1, h]))
-            return carry
-        lax.fori_loop(first, BLOCKS, step, 0)
+        on_blocks(step)
 
     def trailing2(h):
-        first = jnp.where(solver, 1, 0)
         sl = slice(h * HALF, (h + 1) * HALF)
 
-        def step(l, carry):
+        def step(l):
             out[l, 0, :, sl] = out[l, 0, :, sl] - dot(fac[l, :, 2 * NB:3 * NB], w[2, h])
-            return carry
-        lax.fori_loop(first, BLOCKS, step, 0)
-
-    def rest_loaded():
-        for copy in loads[2:]:
-            copy.wait()
-
-    for j in range(CHUNKS):
-        @pl.when(r == 0)
-        def _():
+        on_blocks(step)
+
+    @pl.when(r == 0)
+    def _():
+        for j in range(CHUNKS):
             emit(0, j, c[:, cols(j)])
-        arrive(0, j)
-        forward(0, j)
-
-        @pl.when(r == 1)
-        def _():
+            to_mate(0, j).start()
+            forward(0, j, 0)
+
+    @pl.when(r == 1)
+    def _():
+        for j in range(CHUNKS):
+            arrive(0, j)
             wj = wcols(0, j)
             emit(1, j, c[:, cols(j)] - (dot(m0h[...], wj) + dot(m0l[...], wj)))
-
-        @pl.when(r != 0)
-        def _():
+            forward(1, j, 1)
+            to_mate(1, j).start()
+
+    @pl.when(r == 2)
+    def _():
+        for j in range(CHUNKS):
+            arrive(0, j)
+            to_mate(0, j).start()
             arrive(1, j)
-            forward(1, j)
-
-        @pl.when(r == 2)
-        def _():
+            to_mate(1, j).start()
             w0, w1 = wcols(0, j), wcols(1, j)
             emit(2, j, c[:, cols(j)] - ((dot(m0h[...], w0) + dot(m0l[...], w0))
                                        + (dot(m1h[...], w1) + dot(m1l[...], w1))))
-            forward(2, j)
-
-    @pl.when(r == 0)
-    def _():
-        for j in range(CHUNKS):
-            arrive(1, j)
+            forward(2, j, 2)
+            to_mate(2, j).start()
+
+    @pl.when(even & (r >= 4) & (r <= 8))
+    def _():
+        for j in range(CHUNKS):
+            for p in range(2):
+                arrive(p, j)
+                forward(p, j, 4, 6, 8)
+                to_mate(p, j).start()
+
+    def from_two(js):
+        @pl.when(even & (r >= 10))
+        def _():
+            for j in js:
+                for p in range(2):
+                    arrive(p, j)
+                    to_mate(p, j).start()
+
+        @pl.when(odd & (r >= 3))
+        def _():
+            for j in js:
+                for p in range(2):
+                    arrive(p, j)
+
+        @pl.when(r == 0)
+        def _():
+            for j in js:
+                arrive(1, j)
+
+    def passing(js):
+        for j in js:
+            arrive(2, j)
+            forward(2, j, 1, 11)
+
+            @pl.when(r != 3)
+            def _():
+                to_mate(2, j).start()
 
     def dcopy(k):
         return pltpu.make_async_remote_copy(
@@ -255,22 +286,23 @@
 
     @pl.when(solver)
     def _():
+        dsend[...] = jnp.zeros_like(dsend)
+        dsend[0:1, 0:DPART] = pdiag[...].reshape(1, DPART)
+        dsend[1:2, 0:DPART] = poff[...].reshape(1, DPART)
         for k in range(1, FIELDS):
             dcopy(k).start()
 
-    rest_loaded()
+    for copy in loads[2:]:
+        copy.wait()
+
+    @pl.when(r == 11)
+    def _():
+        passing(range(CHUNKS))
+
+    from_two((0, 1))
     trailing01(0)
+    from_two((2, 3))
     trailing01(1)
-
-    for j in range(CHUNKS):
-        @pl.when(r != 2)
-        def _():
-            arrive(2, j)
-            forward(2, j)
-        if j == 1:
-            trailing2(0)
-
-    trailing2(1)
 
     @pl.when(solver)
     def _():
@@ -311,6 +343,22 @@
             out[0, 0, :, cols(j)] = (own_k * z + next_k * pltpu.roll(z, NB - 1, 0)
                                      + prior_k * pltpu.roll(z, 1, 0))
 
+    @pl.when(r == 1)
+    def _():
+        passing(range(CHUNKS))
+
+    plain = odd & (r != 1) & (r != 11)
+    for h in range(2):
+        @pl.when(plain)
+        def _():
+            passing((2 * h, 2 * h + 1))
+
+        @pl.when(even & (r != 2))
+        def _():
+            for j in (2 * h, 2 * h + 1):
+                arrive(2, j)
+        trailing2(h)
+
     for p in range(PANELS):
         for j in range(CHUNKS):
             for src, dsts in ICI[p]:
@@ -326,11 +374,13 @@
 
 def local(rhs, factor, pivot_map, pivot_diag, pivot_off, perm):
     vmem = pl.BlockSpec(memory_space=pltpu.VMEM)
+    args = [pltpu.with_memory_space_constraint(a, pltpu.HBM)
+            for a in (rhs, factor, pivot_map, pivot_diag, pivot_off, perm)]
     hbm = pl.BlockSpec(memory_space=pltpu.HBM)
     return pl.pallas_call(
         kernel,
         out_shape=jax.ShapeDtypeStruct((BLOCKS, 1, NB, NB), F32),
-        in_specs=[hbm, hbm, vmem, vmem, vmem, vmem],
+        in_specs=[hbm] * 6,
         out_specs=vmem,
         scratch_shapes=[
             pltpu.VMEM((BLOCKS, NB, PANELS * NB), BF16),
@@ -342,7 +392,10 @@
             pltpu.VMEM((NB, NB), BF16), pltpu.VMEM((NB, NB), BF16),
             pltpu.VMEM((NB, 128), F32),
             pltpu.VMEM((8, 256), F32), pltpu.VMEM((FIELDS, 8, 256), F32),
+            pltpu.VMEM((PANELS * NB,), jnp.int32), pltpu.VMEM((DPART,), F32), pltpu.VMEM((DPART,), F32),
+            pltpu.VMEM((PANELS, NB), jnp.int32),
             pltpu.SemaphoreType.DMA((2, BLOCKS)),
+            pltpu.SemaphoreType.DMA((4,)),
             pltpu.SemaphoreType.DMA((PANELS, CHUNKS, 4)),
             pltpu.SemaphoreType.DMA((PANELS, CHUNKS)),
             pltpu.SemaphoreType.DMA((PANELS, CHUNKS)),
@@ -351,7 +404,7 @@
         compiler_params=pltpu.CompilerParams(
             collective_id=0, has_side_effects=True, vmem_limit_bytes=38 << 20),
         cost_estimate=pl.CostEstimate(flops=2 * 4096 * 1536 * 512, bytes_accessed=24 << 20, transcendentals=0),
-    )(rhs, factor, pivot_map, pivot_diag, pivot_off, perm)
+    )(*args)
 
 
 def solution(mesh):

time: 60 us -> 42.1 us (0.70)
  the two profiles are of different devices: /device:TPU:103 before, /device:TPU:116 now
where the time goes in v2:
time: 42.1 us; the launch traced here: 42 us
  Pallas kernels  38.6 us (92%)
  local copies, waits for them, and re-layouts  3.4 us (8%)
    pallas_call x1, Pallas kernels, local(): pl.pallas_call(kernel, out_shape=jax.ShapeDtypeStruct((BLOCKS, 1, NB, NB)...  38.6 us
    unnamed x1, local copies, waits for them, and re-layouts  3.4 us

profile of v2, /device:TPU:116, one launch (start us, length us, event | category | flops | bytes accessed | tf_op | source)
XLA Modules:
  0.0 42.0 jit_solution(10809245741069433729)
XLA Ops:
  0.0 38.6 %shard_map.64 = f32[8,1,512,512]{3,2,1,0:T(8,128)S(1)} custom-call(bf16[8,1,512,512]{3,2,1,0:T(8,128)(2,1)} %rhs.1, bf16[8,1,512,1536]{3,2,1,0:T(8,128)(2,1)} %factor.1, s32[1536]{0:T(1024)} %pmap_hbm.1, f32[192]{0:T(256)} %pdiag_hbm.1, f32[192]{0:T(256)} %poff_hbm.1, s32[3,512]{1,0:T(4,128)} %perm_hbm.1), custom_call_target="tpu_custom_call" | custom-call | flops 6442450944 | bytes 25165824 | tf_op jit(solution)/shard_map/pallas_call | solution.py:380
  38.6 3.4 %copy.8 = f32[8,1,512,512]{3,2,1,0:T(8,128)} copy(f32[8,1,512,512]{3,2,1,0:T(8,128)S(1)} %shard_map.64) | data formatting | bytes 16777216

commit v3 on v2

--- a/solution.py
+++ b/solution.py
@@ -13,6 +13,32 @@
 CHUNKS = 4
 FIELDS, ROWS = 8, 16
 DPART = 192
+
+SENDS = {
+    (0, 0): {0: (1,), 1: (3, 2, 5), 3: (7,), 5: (6, 4)},
+    (0, 1): {0: (3,), 1: (2,), 3: (1, 4, 7), 4: (6,), 7: (5,)},
+    (0, 2): {0: (3,), 3: (1, 2, 7), 7: (4, 6, 5)},
+    (0, 3): {0: (4,), 3: (2, 6), 4: (3, 1, 5, 7)},
+    (1, 0): {0: (4, 1), 1: (2, 5), 2: (3, 6), 4: (7,)},
+    (1, 1): {0: (6, 3, 1), 1: (2,), 3: (4, 7), 4: (5,)},
+    (1, 2): {0: (3, 1), 3: (4, 5, 2, 7), 7: (6,)},
+    (1, 3): {0: (4, 1), 4: (7, 2, 3, 5), 7: (6,)},
+    (2, 0): {0: (3, 4), 1: (0, 2, 5), 5: (6, 7)},
+    (2, 1): {0: (3, 4), 1: (0, 5, 2), 5: (6, 7)},
+    (2, 2): {0: (3, 4), 1: (0, 5, 2), 5: (6, 7)},
+    (2, 3): {0: (3, 4), 1: (0, 5, 2), 5: (6, 7)},
+}
+TAKES = {
+    1: ((0, 0), (1, 0), (1, 1), (0, 1), (1, 2), (0, 3), (0, 2), (1, 3)),
+    2: ((0, 0), (1, 0), (0, 2), (1, 1), (1, 3), (0, 1), (1, 2), (0, 3)),
+    3: ((0, 1), (0, 2), (1, 1), (1, 2), (0, 3), (0, 0), (1, 0), (1, 3)),
+    4: ((0, 3), (1, 0), (1, 3), (0, 1), (1, 1), (0, 0), (1, 2), (0, 2)),
+    5: ((0, 0), (1, 0), (0, 3), (1, 3), (0, 1), (1, 2), (0, 2), (1, 1)),
+    6: ((1, 1), (0, 0), (1, 0), (0, 2), (0, 1), (1, 2), (0, 3), (1, 3)),
+    7: ((0, 1), (0, 2), (0, 3), (1, 1), (1, 0), (1, 2), (1, 3), (0, 0)),
+}
+HUB_STAGE = 0
+FIRST_SENT = (0, 1, 3, 2)
 
 
 def dot(a, b):
@@ -64,7 +90,7 @@
 
 def kernel(rhs, factor, pmap_hbm, pdiag_hbm, poff_hbm, perm_hbm, out, fac, b, w, xh, xl, c,
            m0h, m0l, m1h, m1l, coef, dsend, dall, pmap, pdiag, poff, perm,
-           load_sem, small_sem, send_sem, recv_sem, core_sem, dsend_sem, drecv_sem):
+           load_sem, small_sem, send_sem, recv_sem, dsend_sem, drecv_sem):
     r = lax.axis_index("row")
     f = lax.axis_index("field")
     even = lax.rem(r, 2) == 0
@@ -72,10 +98,10 @@
     solver = r < PANELS
     mate = r + 1 - 2 * lax.rem(r, 2)
 
-    loads = []
-    for l in range(BLOCKS):
-        loads.append(pltpu.make_async_copy(factor.at[l, 0], fac.at[l], load_sem.at[0, l]))
-        loads.append(pltpu.make_async_copy(rhs.at[l, 0], b.at[l], load_sem.at[1, l]))
+    rest = pl.ds(1, BLOCKS - 1)
+    loads = [pltpu.make_async_copy(src, dst, load_sem.at[k]) for k, (src, dst) in enumerate(
+        ((factor.at[0, 0], fac.at[0]), (rhs.at[0, 0], b.at[0]),
+         (factor.at[rest, 0], fac.at[rest]), (rhs.at[rest, 0], b.at[rest])))]
     small = [pltpu.make_async_copy(src, dst, small_sem.at[k]) for k, (src, dst) in enumerate(
         ((perm_hbm, perm), (pmap_hbm, pmap), (pdiag_hbm, pdiag), (poff_hbm, poff)))]
     loads[0].start()
@@ -95,37 +121,39 @@
     def wslot(p, j):
         return w.at[p, j // 2, :, pl.ds((j % 2) * CHUNK, CHUNK)]
 
-    def send(p, j, k, dst):
+    started = [[] for _ in range(ROWS)]
+
+    def remote(p, j, k, dst):
         return pltpu.make_async_remote_copy(
-            wslot(p, j), wslot(p, j), send_sem.at[p, j, k], recv_sem.at[p, j],
+            wslot(p, j), wslot(p, j), send_sem.at[k], recv_sem.at[p, j],
             device_id=(dst, f), device_id_type=MESH)
 
-    def to_mate(p, j):
-        return pltpu.make_async_remote_copy(
-            wslot(p, j), wslot(p, j), core_sem.at[p, j], recv_sem.at[p, j],
-            device_id=(mate, f), device_id_type=MESH)
-
-    EARLY = ((6, (4, 14)), (4, (12,)), (8, (10,)))
-    ICI = [((0, (2, 6, 8)),) + EARLY, ((1, (2, 6, 8)),) + EARLY,
-           ((2, (11, 1, 5)), (1, (7, 9)), (11, (15, 13)))]
-
-    def core_sender(p):
-        if p == 0:
-            return even
-        if p == 1:
-            return (r == 1) | (even & (r > 0))
-        return (r == 2) | (odd & (r != 3))
-
-    def forward(p, j, *rows):
-        for src, dsts in ICI[p]:
-            if src in rows:
-                @pl.when(r == src)
-                def _():
-                    for k, dst in enumerate(dsts):
-                        send(p, j, k, dst).start()
+    def start(row, p, j, dst):
+        remote(p, j, len(started[row]), dst).start()
+        started[row].append((p, j, dst))
+
+    def start_mate(row, p, j):
+        start(row, p, j, row ^ 1)
+
+    def pass_on(row, p, j):
+        owner = row == p
+        if not owner and (row // 2 == p // 2 or row % 2 != (1 if p == 2 else 0)):
+            return
+        for chip in SENDS[p, j].get(row // 2, ()):
+            start(row, p, j, 2 * chip + (1 if p == 2 else 0))
 
     def arrive(p, j):
-        to_mate(p, j).wait_recv()
+        remote(p, j, 0, mate).wait_recv()
+
+    def take(row, p, j):
+        arrive(p, j)
+        pass_on(row, p, j)
+        if p == 2:
+            relay = row % 2 == 1 and row != 3
+        else:
+            relay = row % 2 == 0 and row > 0
+        if relay:
+            start_mate(row, p, j)
 
     for copy in small + loads[:2]:
         copy.wait()
@@ -210,10 +238,10 @@
 
     @pl.when(r == 0)
     def _():
-        for j in range(CHUNKS):
+        for j in FIRST_SENT:
             emit(0, j, c[:, cols(j)])
-            to_mate(0, j).start()
-            forward(0, j, 0)
+            start_mate(0, 0, j)
+            pass_on(0, 0, j)
 
     @pl.when(r == 1)
     def _():
@@ -221,57 +249,58 @@
             arrive(0, j)
             wj = wcols(0, j)
             emit(1, j, c[:, cols(j)] - (dot(m0h[...], wj) + dot(m0l[...], wj)))
-            forward(1, j, 1)
-            to_mate(1, j).start()
+            pass_on(1, 1, j)
+            start_mate(1, 1, j)
 
     @pl.when(r == 2)
     def _():
-        for j in range(CHUNKS):
-            arrive(0, j)
-            to_mate(0, j).start()
-            arrive(1, j)
-            to_mate(1, j).start()
-            w0, w1 = wcols(0, j), wcols(1, j)
-            emit(2, j, c[:, cols(j)] - ((dot(m0h[...], w0) + dot(m0l[...], w0))
-                                       + (dot(m1h[...], w1) + dot(m1l[...], w1))))
-            forward(2, j, 2)
-            to_mate(2, j).start()
-
-    @pl.when(even & (r >= 4) & (r <= 8))
-    def _():
-        for j in range(CHUNKS):
-            for p in range(2):
-                arrive(p, j)
-                forward(p, j, 4, 6, 8)
-                to_mate(p, j).start()
-
-    def from_two(js):
-        @pl.when(even & (r >= 10))
-        def _():
-            for j in js:
-                for p in range(2):
-                    arrive(p, j)
-                    to_mate(p, j).start()
-
-        @pl.when(odd & (r >= 3))
-        def _():
-            for j in js:
-                for p in range(2):
-                    arrive(p, j)
-
-        @pl.when(r == 0)
-        def _():
-            for j in js:
-                arrive(1, j)
-
-    def passing(js):
-        for j in js:
-            arrive(2, j)
-            forward(2, j, 1, 11)
-
-            @pl.when(r != 3)
-            def _():
-                to_mate(2, j).start()
+        here = set()
+        sent = 0
+        for p, j in TAKES[1]:
+            take(2, p, j)
+            here.add((p, j))
+            while (0, sent) in here and (1, sent) in here:
+                w0, w1 = wcols(0, sent), wcols(1, sent)
+                emit(2, sent, c[:, cols(sent)] - ((dot(m0h[...], w0) + dot(m0l[...], w0))
+                                                  + (dot(m1h[...], w1) + dot(m1l[...], w1))))
+                pass_on(2, 2, sent)
+                start_mate(2, 2, sent)
+                sent += 1
+
+    stages = [[[] for _ in range(4)] for _ in range(ROWS)]
+    last = [(2, j) for j in range(CHUNKS)]
+    stages[0][0] = [(1, j) for j in range(CHUNKS)]
+    for chip in range(8):
+        low, high = 2 * chip, 2 * chip + 1
+        if chip > 0:
+            halves = [[x for x in TAKES[chip] if x[1] // 2 == h] for h in range(2)]
+            passes = any(chip in SENDS[x] for x in TAKES[chip])
+            if chip > 1:
+                if passes:
+                    stages[low][0] += TAKES[chip]
+                else:
+                    stages[low][0] += halves[0]
+                    stages[low][1] += halves[1]
+            stages[high][0] += halves[0]
+            stages[high][1] += halves[1]
+        hub = chip != 1 and any(chip in SENDS[x] for x in last)
+        if hub:
+            at = 2 if chip == 0 else HUB_STAGE
+            stages[high][at] = last + stages[high][at]
+        else:
+            stages[high][2] += last[:2]
+            stages[high][3] += last[2:]
+        if chip != 1:
+            stages[low][2] += last[:2]
+            stages[low][3] += last[2:]
+
+    def run_stage(k):
+        for row in range(ROWS):
+            if stages[row][k]:
+                @pl.when(r == row)
+                def _():
+                    for p, j in stages[row][k]:
+                        take(row, p, j)
 
     def dcopy(k):
         return pltpu.make_async_remote_copy(
@@ -295,13 +324,9 @@
     for copy in loads[2:]:
         copy.wait()
 
-    @pl.when(r == 11)
-    def _():
-        passing(range(CHUNKS))
-
-    from_two((0, 1))
+    run_stage(0)
     trailing01(0)
-    from_two((2, 3))
+    run_stage(1)
     trailing01(1)
 
     @pl.when(solver)
@@ -343,33 +368,19 @@
             out[0, 0, :, cols(j)] = (own_k * z + next_k * pltpu.roll(z, NB - 1, 0)
                                      + prior_k * pltpu.roll(z, 1, 0))
 
-    @pl.when(r == 1)
-    def _():
-        passing(range(CHUNKS))
-
-    plain = odd & (r != 1) & (r != 11)
-    for h in range(2):
-        @pl.when(plain)
+    run_stage(2)
+    trailing2(0)
+    run_stage(3)
+    trailing2(1)
+
+    for row in range(ROWS):
+        @pl.when(r == row)
         def _():
-            passing((2 * h, 2 * h + 1))
-
-        @pl.when(even & (r != 2))
-        def _():
-            for j in (2 * h, 2 * h + 1):
-                arrive(2, j)
-        trailing2(h)
-
-    for p in range(PANELS):
-        for j in range(CHUNKS):
-            for src, dsts in ICI[p]:
-                @pl.when(r == src)
-                def _():
-                    for k, dst in enumerate(dsts):
-                        send(p, j, k, dst).wait_send()
-
-            @pl.when(core_sender(p))
-            def _():
-                to_mate(p, j).wait_send()
+            for k, (p, j, dst) in enumerate(started[row]):
+                remote(p, j, k, dst).wait_send()
+
+
+MAX_SENDS = 31
 
 
 def local(rhs, factor, pivot_map, pivot_diag, pivot_off, perm):
@@ -394,10 +405,9 @@
             pltpu.VMEM((8, 256), F32), pltpu.VMEM((FIELDS, 8, 256), F32),
             pltpu.VMEM((PANELS * NB,), jnp.int32), pltpu.VMEM((DPART,), F32), pltpu.VMEM((DPART,), F32),
             pltpu.VMEM((PANELS, NB), jnp.int32),
-            pltpu.SemaphoreType.DMA((2, BLOCKS)),
             pltpu.SemaphoreType.DMA((4,)),
-            pltpu.SemaphoreType.DMA((PANELS, CHUNKS, 4)),
-            pltpu.SemaphoreType.DMA((PANELS, CHUNKS)),
+            pltpu.SemaphoreType.DMA((4,)),
+            pltpu.SemaphoreType.DMA((MAX_SENDS,)),
             pltpu.SemaphoreType.DMA((PANELS, CHUNKS)),
             pltpu.SemaphoreType.DMA((FIELDS,)), pltpu.SemaphoreType.DMA((FIELDS,)),
         ],

time: 42.1 us -> 37.8 us (0.90)
  Pallas kernels: 38.6 us -> 34.2 us
    pallas_call x1, Pallas kernels: 38.6 us -> 34.2 us  [local(): pl.pallas_call(kernel, out_shape=jax.ShapeDtypeStruct((BLOCKS, 1, NB, NB)...]
where the time goes in v3:
time: 37.8 us; the launch traced here: 37.6 us
  Pallas kernels  34.2 us (90%)
  local copies, waits for them, and re-layouts  3.4 us (9%)
    pallas_call x1, Pallas kernels, local(): pl.pallas_call(kernel, out_shape=jax.ShapeDtypeStruct((BLOCKS, 1, NB, NB)...  34.2 us
    unnamed x1, local copies, waits for them, and re-layouts  3.4 us

profile of v3, /device:TPU:116, one launch (start us, length us, event | category | flops | bytes accessed | tf_op | source)
XLA Modules:
  0.0 37.6 jit_solution(3968749634917657462)
XLA Ops:
  0.0 34.2 %shard_map.64 = f32[8,1,512,512]{3,2,1,0:T(8,128)S(1)} custom-call(bf16[8,1,512,512]{3,2,1,0:T(8,128)(2,1)} %rhs.1, bf16[8,1,512,1536]{3,2,1,0:T(8,128)(2,1)} %factor.1, s32[1536]{0:T(1024)} %pmap_hbm.1, f32[192]{0:T(256)} %pdiag_hbm.1, f32[192]{0:T(256)} %poff_hbm.1, s32[3,512]{1,0:T(4,128)} %perm_hbm.1), custom_call_target="tpu_custom_call" | custom-call | flops 6442450944 | bytes 25165824 | tf_op jit(solution)/shard_map/pallas_call | solution.py:391
  34.2 3.4 %copy.8 = f32[8,1,512,512]{3,2,1,0:T(8,128)} copy(f32[8,1,512,512]{3,2,1,0:T(8,128)S(1)} %shard_map.64) | data formatting | bytes 16777216

commit v4 on v3

--- a/solution.py
+++ b/solution.py
@@ -15,30 +15,30 @@
 DPART = 192
 
 SENDS = {
-    (0, 0): {0: (1,), 1: (3, 2, 5), 3: (7,), 5: (6, 4)},
-    (0, 1): {0: (3,), 1: (2,), 3: (1, 4, 7), 4: (6,), 7: (5,)},
-    (0, 2): {0: (3,), 3: (1, 2, 7), 7: (4, 6, 5)},
-    (0, 3): {0: (4,), 3: (2, 6), 4: (3, 1, 5, 7)},
-    (1, 0): {0: (4, 1), 1: (2, 5), 2: (3, 6), 4: (7,)},
-    (1, 1): {0: (6, 3, 1), 1: (2,), 3: (4, 7), 4: (5,)},
-    (1, 2): {0: (3, 1), 3: (4, 5, 2, 7), 7: (6,)},
-    (1, 3): {0: (4, 1), 4: (7, 2, 3, 5), 7: (6,)},
+    (0, 0): {0: (3,), 3: (1, 7, 4, 6, 2), 7: (5,)},
+    (0, 1): {0: (1,), 1: (5, 7, 2, 4), 2: (3,), 5: (6,)},
+    (0, 2): {0: (4,), 3: (2,), 4: (1, 3, 5), 5: (7, 6)},
+    (0, 3): {0: (4, 1), 1: (5, 2), 2: (3,), 4: (6, 7)},
+    (1, 0): {0: (1, 7), 1: (2,), 7: (6, 3, 5, 4)},
+    (1, 1): {0: (2, 7, 1), 2: (3, 6), 7: (5, 4)},
+    (1, 2): {0: (1, 4), 4: (7, 2, 5), 7: (6, 3)},
+    (1, 3): {0: (3, 1, 4), 3: (2,), 4: (7, 5), 7: (6,)},
     (2, 0): {0: (3, 4), 1: (0, 2, 5), 5: (6, 7)},
-    (2, 1): {0: (3, 4), 1: (0, 5, 2), 5: (6, 7)},
-    (2, 2): {0: (3, 4), 1: (0, 5, 2), 5: (6, 7)},
-    (2, 3): {0: (3, 4), 1: (0, 5, 2), 5: (6, 7)},
+    (2, 1): {0: (3, 4), 1: (2, 5, 0), 5: (7, 6)},
+    (2, 2): {0: (4, 3), 1: (0, 2, 5), 5: (6, 7)},
+    (2, 3): {0: (4, 3), 1: (5, 2, 0), 5: (7, 6)},
 }
 TAKES = {
-    1: ((0, 0), (1, 0), (1, 1), (0, 1), (1, 2), (0, 3), (0, 2), (1, 3)),
-    2: ((0, 0), (1, 0), (0, 2), (1, 1), (1, 3), (0, 1), (1, 2), (0, 3)),
-    3: ((0, 1), (0, 2), (1, 1), (1, 2), (0, 3), (0, 0), (1, 0), (1, 3)),
-    4: ((0, 3), (1, 0), (1, 3), (0, 1), (1, 1), (0, 0), (1, 2), (0, 2)),
-    5: ((0, 0), (1, 0), (0, 3), (1, 3), (0, 1), (1, 2), (0, 2), (1, 1)),
-    6: ((1, 1), (0, 0), (1, 0), (0, 2), (0, 1), (1, 2), (0, 3), (1, 3)),
-    7: ((0, 1), (0, 2), (0, 3), (1, 1), (1, 0), (1, 2), (1, 3), (0, 0)),
+    1: ((0, 1), (0, 3), (1, 0), (0, 0), (1, 1), (0, 2), (1, 2), (1, 3)),
+    2: ((1, 1), (0, 1), (0, 0), (0, 3), (1, 0), (1, 3), (0, 2), (1, 2)),
+    3: ((0, 0), (1, 3), (0, 2), (1, 0), (1, 1), (0, 1), (0, 3), (1, 2)),
+    4: ((0, 2), (0, 3), (1, 2), (1, 3), (1, 0), (0, 0), (1, 1), (0, 1)),
+    5: ((0, 1), (0, 3), (0, 2), (1, 0), (1, 1), (1, 2), (0, 0), (1, 3)),
+    6: ((0, 0), (1, 0), (0, 3), (1, 1), (0, 1), (0, 2), (1, 2), (1, 3)),
+    7: ((1, 0), (1, 1), (0, 0), (0, 3), (0, 1), (1, 2), (1, 3), (0, 2)),
 }
 HUB_STAGE = 0
-FIRST_SENT = (0, 1, 3, 2)
+FIRST_SENT = (0, 1, 2, 3)
 
 
 def dot(a, b):

time: 37.8 us -> 45 us (1.19)
  Pallas kernels: 34.2 us -> 41.5 us
    pallas_call x1, Pallas kernels: 34.2 us -> 41.5 us  [local(): pl.pallas_call(kernel, out_shape=jax.ShapeDtypeStruct((BLOCKS, 1, NB, NB)...]
where the time goes in v4:
time: 45 us; the launch traced here: 44.9 us
  Pallas kernels  41.5 us (92%)
  local copies, waits for them, and re-layouts  3.4 us (8%)
    pallas_call x1, Pallas kernels, local(): pl.pallas_call(kernel, out_shape=jax.ShapeDtypeStruct((BLOCKS, 1, NB, NB)...  41.5 us
    unnamed x1, local copies, waits for them, and re-layouts  3.4 us

profile of v4, /device:TPU:116, one launch (start us, length us, event | category | flops | bytes accessed | tf_op | source)
XLA Modules:
  0.0 44.9 jit_solution(6174187894410483344)
XLA Ops:
  0.0 41.5 %shard_map.64 = f32[8,1,512,512]{3,2,1,0:T(8,128)S(1)} custom-call(bf16[8,1,512,512]{3,2,1,0:T(8,128)(2,1)} %rhs.1, bf16[8,1,512,1536]{3,2,1,0:T(8,128)(2,1)} %factor.1, s32[1536]{0:T(1024)} %pmap_hbm.1, f32[192]{0:T(256)} %pdiag_hbm.1, f32[192]{0:T(256)} %poff_hbm.1, s32[3,512]{1,0:T(4,128)} %perm_hbm.1), custom_call_target="tpu_custom_call" | custom-call | flops 6442450944 | bytes 25165824 | tf_op jit(solution)/shard_map/pallas_call | solution.py:391
  41.5 3.4 %copy.8 = f32[8,1,512,512]{3,2,1,0:T(8,128)} copy(f32[8,1,512,512]{3,2,1,0:T(8,128)S(1)} %shard_map.64) | data formatting | bytes 16777216
